TPU v7x, 32 devices: a whole 2x2x4 slice. The times are simulated.
32 devices in a mesh: db: 16 (over z, y, x), seq: 2 (over core).
Axes of the slice: x: 2, y: 2, z: 4, core: 2. Of those that a mesh axis runs over, the one named last changes fastest.
Arguments:
- reader: bfloat16 [16, 256, 2048], P('db', 'seq'), may hold values from -6 to 6
- reader_gain: float32 [2048], replicated, may hold values from 0.1 to 1.9
- database: bfloat16 [512, 8, 896], P('db')
- encoder_gain: float32 [896], replicated, may hold values from 0.1 to 1.9
- w_expand: bfloat16 [896, 1792], P('db', 'seq'), may hold values from -0.1875 to 0.1875
- w_reduce: bfloat16 [1792, 896], P('seq', 'db'), may hold values from -0.125 to 0.125
- w_query: bfloat16 [2048, 2048], P('db', 'seq'), may hold values from -0.125 to 0.125
- w_key: bfloat16 [896, 2048], P('db', 'seq'), may hold values from -0.1875 to 0.1875
- w_value: bfloat16 [896, 2048], P('db', 'seq'), may hold values from -0.1875 to 0.1875
- w_output: bfloat16 [2048, 2048], P('db', 'seq'), may hold values from -0.125 to 0.125
- neighbour_ids: int32 [16, 2, 4], replicated, may hold values from 0 to 31
- lengths: int32 [16, 2, 4], P('db'), may hold values from 1 to 128, 320 in all within a row
- owners: int32 [16, 2, 4], P('db'), may hold values from 0 to 15
Outputs:
- updated: bfloat16 [16, 256, 2048], P('db', None, 'seq')
Inputs may be any that keep to these rules, and one draw needn't show every extreme that they name: For every sequence b and every q, the lengths[b, q, :] of its 4 neighbours sum to exactly 320, and the longest of them is 128.
All inputs are finite; a program needn't handle non-finite values.
Results may differ from a plain program's by a relative error of at most 0.0065.
The roundings to bfloat16 on the way count: a program that leaves them out, or rounds other values in their place, can miss the bound.
Values may be sent and summed in bfloat16 or wider, within the bound.
A program may use at most 64 MiB of HBM per device.

v0:
```python
import jax
import jax.numpy as jnp
from jax import lax
from jax.sharding import PartitionSpec as P

HD = 128
SPAN = 64
KNN = 2


epsilon = 1e-06


def rms_scale(values, scales):
    widened = values.astype(jnp.float32)
    mean_square = jnp.mean(widened * widened, axis=-1, keepdims=True)
    return widened * lax.rsqrt(mean_square + epsilon) * scales


def body(
    reader,
    reader_gain,
    database,
    encoder_gain,
    w_expand,
    w_reduce,
    w_query,
    w_key,
    w_value,
    w_output,
    neighbour_ids,
    lengths,
    owners,
):
    shards = lax.axis_size("db")
    seq_index = lax.axis_index("seq")
    entries, stripe, features = database.shape
    query_part = lax.all_gather(w_query, "db", axis=0, tiled=True)
    reader_output_part = lax.all_gather(w_output, "db", axis=0, tiled=True)
    rows = lax.all_gather(reader[0], "seq", axis=0, tiled=True)
    normed_tokens = rms_scale(rows, reader_gain).astype(jnp.bfloat16)
    queries = jnp.dot(normed_tokens, query_part, preferred_element_type=jnp.float32).astype(
        jnp.bfloat16
    )
    rows, queries, output_part = (rows, queries, reader_output_part)
    expand_part = lax.all_gather(w_expand, "db", axis=0, tiled=True)
    reduce_part = lax.all_gather(w_reduce, "db", axis=1, tiled=True)
    key_part = lax.all_gather(w_key, "db", axis=0, tiled=True)
    value_part = lax.all_gather(w_value, "db", axis=0, tiled=True)
    stored = database.reshape(entries * stripe, features)
    normed_rows = rms_scale(stored, encoder_gain).astype(jnp.bfloat16)
    hidden = jax.nn.gelu(
        jnp.dot(normed_rows, expand_part, preferred_element_type=jnp.float32), approximate=False
    ).astype(jnp.bfloat16)
    partial_sum = jnp.dot(hidden, reduce_part, preferred_element_type=jnp.float32)
    total = lax.psum(partial_sum, "seq")
    encoded = (stored.astype(jnp.float32) + total).astype(jnp.bfloat16)
    w_pairs = jnp.concatenate([key_part, value_part], axis=1)
    table = jnp.dot(encoded, w_pairs, preferred_element_type=jnp.float32).astype(jnp.bfloat16)
    table = table.reshape(entries, stripe, w_pairs.shape[1])
    requests = neighbour_ids.reshape(shards, -1)
    outgoing = table[requests]
    arrived = lax.all_to_all(outgoing, "db", split_axis=0, concat_axis=0, tiled=True)
    seq_len = rows.shape[0]
    per_seq = neighbour_ids.shape[1] * neighbour_ids.shape[2]
    width = arrived.shape[-1]
    local_heads = width // (2 * HD)
    positions = jnp.arange(stripe * shards, dtype=jnp.int32)
    owner_flat = owners[0].reshape(-1)
    length_flat = lengths[0].reshape(-1)
    source = (owner_flat[:, None] + positions[None, :] // stripe) % shards
    neighbour_index = jnp.arange(per_seq, dtype=jnp.int32)[:, None]
    flat_index = (source * per_seq + neighbour_index) * stripe + (positions % stripe)[None, :]
    key_value = arrived.reshape(-1, width)[flat_index]
    live = positions[None, :] < length_flat[:, None]
    spans = per_seq // KNN
    window = KNN * positions.shape[0]
    span_pairs = key_value.reshape(spans, window, width)
    span_live = live.reshape(spans, window)
    prior_pairs = jnp.concatenate(
        [jnp.zeros((1, window, width), jnp.bfloat16), span_pairs[:-1]], axis=0
    )
    prior_live = jnp.concatenate([jnp.zeros((1, window), bool), span_live[:-1]], axis=0)
    query_spans = queries.reshape(spans, SPAN, local_heads, HD)
    key_heads = prior_pairs[:, :, : local_heads * HD].reshape(spans, window, local_heads, HD)
    value_heads = prior_pairs[:, :, local_heads * HD :].reshape(spans, window, local_heads, HD)
    scores = jnp.einsum(
        "cqhd,ckhd->chqk", query_spans, key_heads, preferred_element_type=jnp.float32
    ) * HD ** (-0.5)
    masked = jnp.where(prior_live[:, None, None, :], scores, -jnp.inf)
    largest = jnp.max(masked, axis=-1, keepdims=True)
    largest = jnp.where(jnp.isfinite(largest), largest, 0.0)
    powers = jnp.exp(masked - largest)
    totals = jnp.sum(powers, axis=-1, keepdims=True)
    weights = (powers / jnp.where(totals > 0, totals, 1.0)).astype(jnp.bfloat16)
    attended = jnp.einsum(
        "chqk,ckhd->cqhd", weights, value_heads, preferred_element_type=jnp.float32
    )
    attended = attended.reshape(seq_len, local_heads * HD).astype(jnp.bfloat16)
    model_cols = output_part.shape[1]
    update = jnp.dot(
        lax.all_gather(attended, "seq", axis=1, tiled=True),
        output_part,
        preferred_element_type=jnp.float32,
    )
    residual = lax.dynamic_slice_in_dim(rows, seq_index * model_cols, model_cols, 1)
    result = (residual.astype(jnp.float32) + update).astype(jnp.bfloat16)
    return result[None]


def solution(mesh):
    in_specs = (
        P("db", "seq", None),
        P(),
        P("db", None, None),
        P(),
        P("db", "seq"),
        P("seq", "db"),
        P("db", "seq"),
        P("db", "seq"),
        P("db", "seq"),
        P("db", "seq"),
        P(),
        P("db", None, None),
        P("db", None, None),
    )
    out_specs = P("db", None, "seq")
    return jax.shard_map(body, mesh=mesh, in_specs=in_specs, out_specs=out_specs, check_vma=False)
```

profile of v0, /device:TPU:9, one launch (start us, length us, event | category | flops | bytes accessed | tf_op | source)
XLA Modules:
  0.0 518.5 jit_solution(7210015848162929367)
XLA Ops:
  9.4 1.2 fusion.32
  10.7 57.0 %all-gather.12.cloned.1.call-done = bf16[896,896]{0,1:T(8,128)(2,1)} async-done(((bf16[896,56]{0,1:T(8,128)(2,1)}), bf16[896,896]{0,1:T(8,128)(2,1)}) %all-gather.12.cloned.1.call-update) | async-done | bytes 1605648 | tf_op jit(solution)/shard_map/all_gather | solution.py:47
  67.7 59.5 %all-gather.10.cloned.1.call-done = bf16[896,896]{1,0:T(8,128)(2,1)} async-done(((bf16[56,896]{1,0:T(8,128)(2,1)}), bf16[896,896]{1,0:T(8,128)(2,1)}) %all-gather.10.cloned.1.call-update) | async-done | bytes 1605648 | tf_op jit(solution)/shard_map/all_gather | solution.py:46
  127.2 6.0 %fusion.45 = f32[256,896]{1,0:T(8,128)} fusion(bf16[896,896]{0,1:T(8,128)(2,1)} %all-gather.12.cloned.1.call-done, bf16[896,896]{1,0:T(8,128)(2,1)} %all-gather.10.cloned.1.call-done, bf16[32,8,896]{2,1,0:T(8,128)(2,1)} %param.15, f32[896]{0:T(1024)} %param.16, f32[256]{0:T(256)S(1)} %rsqrt.20), kind=kOutput, calls=%fused_computation.64 | convolution fusion | flops 837910528 | bytes 4592128 | tf_op jit(solution)/shard_map/dot_general | solution.py:55
  134.7 53.5 %all-gather.16.cloned.1.call-done = bf16[896,1024]{1,0:T(8,128)(2,1)} async-done(((bf16[56,1024]{1,0:T(8,128)(2,1)}), bf16[896,1024]{1,0:T(8,128)(2,1)}) %all-gather.16.cloned.1.call-update) | async-done | bytes 1835024 | tf_op jit(solution)/shard_map/all_gather | solution.py:49
  188.2 60.6 %all-gather.14.cloned.1.call-done = bf16[896,1024]{1,0:T(8,128)(2,1)} async-done(((bf16[56,1024]{1,0:T(8,128)(2,1)}), bf16[896,1024]{1,0:T(8,128)(2,1)}) %all-gather.14.cloned.1.call-update) | async-done | bytes 1835024 | tf_op jit(solution)/shard_map/all_gather | solution.py:48
  248.8 22.4 %all-reduce.4.cloned.1.call-done = f32[256,896]{1,0:T(8,128)} async-done(((f32[256,896]{1,0:T(8,128)}), f32[256,896]{1,0:T(8,128)}) %all-reduce.4.cloned.1.call-update) | async-done | bytes 917520 | tf_op jit(solution)/shard_map/psum | solution.py:56
  271.2 3.6 fusion.7
  274.8 2.8 gather_fusion
  277.6 6.5 %all-to-all-start = ((bf16[16,8,8,2048]{3,2,1,0:T(8,128)(2,1)}), bf16[16,8,8,2048]{3,2,1,0:T(8,128)(2,1)}, u32[]{:S(2)}, u32[]{:S(2)}) async-start(bf16[16,8,8,2048]{3,2,1,0:T(8,128)(2,1)} %bitcast.63), calls=%async_computation | async-start | bytes 8388608 | tf_op jit(solution)/shard_map/all_to_all | solution.py:63
  285.5 1.5 fusion.10
  287.0 129.8 %all-gather.18.cloned.1.call-done = bf16[2048,1024]{1,0:T(8,128)(2,1)} async-done(((bf16[128,1024]{1,0:T(8,128)(2,1)}), bf16[2048,1024]{1,0:T(8,128)(2,1)}) %all-gather.18.cloned.1.call-update) | async-done | bytes 4194320 | tf_op jit(solution)/shard_map/all_gather | solution.py:38
  416.9 3.8 fusion.16
  420.7 0.9 copy.24
  421.6 11.6 %gather_fusion.1 = bf16[1024,2048]{1,0:T(8,128)(2,1)} fusion(bf16[1024,2048]{1,0:T(8,128)(2,1)} %bitcast.5, s32[1024]{0:T(1024)S(1)} %fusion.94), kind=kCustom, calls=%fused_computation.1 | custom fusion | bytes 8392704 | tf_op jit(solution)/shard_map/gather | solution.py:74
  433.2 1.9 slice-done
  435.1 2.8 copy.17
  437.9 2.2 pad_slice_fusion
  440.8 0.8 fusion.14
  441.6 1.0 fusion.17
  443.0 0.9 copy.31
  443.9 52.3 %all-gather.22.cloned.1.call-done = bf16[2048,1024]{1,0:T(8,128)(2,1)} async-done(((bf16[128,1024]{1,0:T(8,128)(2,1)}), bf16[2048,1024]{1,0:T(8,128)(2,1)}) %all-gather.22.cloned.1.call-update) | async-done | bytes 4194320 | tf_op jit(solution)/shard_map/all_gather | solution.py:39
  496.2 11.2 %all-gather.20.cloned.1.call-done = bf16[256,2048]{1,0:T(8,128)(2,1)} async-done(((bf16[256,1024]{1,0:T(8,128)(2,1)}), bf16[256,2048]{1,0:T(8,128)(2,1)}) %all-gather.20.cloned.1.call-update) | async-done | bytes 1048592 | tf_op jit(solution)/shard_map/all_gather | solution.py:102
  507.4 4.6 fusion.18
  (53 shorter events, 6.7 us)
Async XLA Ops:
  6.5 61.2 %all-gather.12.cloned.1.call-start = ((), (), s32[]{:S(2)}) async-start(), calls=%async_computation.2 | async-start | bytes 1705984 | tf_op jit(solution)/shard_map/all_gather | solution.py:47
  7.3 119.9 %all-gather.10.cloned.1.call-start = ((), (), s32[]{:S(2)}) async-start(), calls=%async_computation.1 | async-start | bytes 1705984 | tf_op jit(solution)/shard_map/all_gather | solution.py:46
  8.0 180.2 %all-gather.16.cloned.1.call-start = ((), (), s32[]{:S(2)}) async-start(), calls=%async_computation.5 | async-start | bytes 1949696 | tf_op jit(solution)/shard_map/all_gather | solution.py:49
  8.7 240.0 %all-gather.14.cloned.1.call-start = ((), (), s32[]{:S(2)}) async-start(), calls=%async_computation.4 | async-start | bytes 1949696 | tf_op jit(solution)/shard_map/all_gather | solution.py:48
  9.3 261.9 %all-reduce.4.cloned.1.call-start = ((), (), s32[]{:S(2)}) async-start(), calls=%async_computation.3 | async-start | bytes 1835008 | tf_op jit(solution)/shard_map/psum | solution.py:56
  10.7 123.9 %copy-start.3 = (s32[16,2,4]{0,2,1:T(4,128)S(1)}, s32[16,2,4]{0,2,1:T(4,128)}, u32[]{:S(2)}) copy-start(s32[16,2,4]{0,2,1:T(4,128)} %param.23) | copy-start | bytes 1540
  10.7 260.5 %copy-start.2 = (bf16[32,8,896]{2,1,0:T(8,128)(2,1)S(1)}, bf16[32,8,896]{2,1,0:T(8,128)(2,1)}, u32[]{:S(2)}) copy-start(bf16[32,8,896]{2,1,0:T(8,128)(2,1)} %param.15) | copy-start | bytes 1376260
  133.2 152.3 %all-gather.24.cloned.1.call-start = ((), (), s32[]{:S(2)}) async-start(), calls=%async_computation.9 | async-start | bytes 1572864 | tf_op jit(solution)/shard_map/all_gather | solution.py:40
  133.8 283.1 %all-gather.18.cloned.1.call-start = ((), (), s32[]{:S(2)}) async-start(), calls=%async_computation.6 | async-start | bytes 4456448 | tf_op jit(solution)/shard_map/all_gather | solution.py:38
  277.6 7.5 %copy-start.5 = (s32[1,2,4]{2,1,0:T(2,128)S(1)}, s32[1,2,4]{2,1,0:T(2,128)}, u32[]{:S(2)}) copy-start(s32[1,2,4]{2,1,0:T(2,128)} %param.25) | copy-start | bytes 100
  277.6 7.6 %copy-start.6 = (s32[1,2,4]{2,1,0:T(2,128)S(1)}, s32[1,2,4]{2,1,0:T(2,128)}, u32[]{:S(2)}) copy-start(s32[1,2,4]{2,1,0:T(2,128)} %param.24) | copy-start | bytes 100
  277.6 139.3 %copy-start.4 = (f32[2048]{0:T(1024)S(1)}, f32[2048]{0:T(1024)}, u32[]{:S(2)}) copy-start(f32[2048]{0:T(1024)} %param.14) | copy-start | bytes 24580
  277.6 144.0 %all-to-all-start = ((bf16[16,8,8,2048]{3,2,1,0:T(8,128)(2,1)}), bf16[16,8,8,2048]{3,2,1,0:T(8,128)(2,1)}, u32[]{:S(2)}, u32[]{:S(2)}) async-start(bf16[16,8,8,2048]{3,2,1,0:T(8,128)(2,1)} %bitcast.63), calls=%async_computation | async-start | bytes 8388608 | tf_op jit(solution)/shard_map/all_to_all | solution.py:63
  284.1 212.1 %all-gather.22.cloned.1.call-start = ((), (), s32[]{:S(2)}) async-start(), calls=%async_computation.8 | async-start | bytes 4456448 | tf_op jit(solution)/shard_map/all_gather | solution.py:39
  284.9 222.5 %all-gather.20.cloned.1.call-start = ((), (), s32[]{:S(2)}) async-start(), calls=%async_computation.7 | async-start | bytes 1572864 | tf_op jit(solution)/shard_map/all_gather | solution.py:102
  433.2 1.9 slice-start
  437.9 2.2 copy-start
  442.6 64.8 %copy-start.1 = (bf16[1,256,2048]{2,1,0:T(8,128)(2,1)S(1)}, bf16[1,256,2048]{2,1,0:T(8,128)(2,1)}, u32[]{:S(2)}) copy-start(bf16[1,256,2048]{2,1,0:T(8,128)(2,1)} %all-gather.24.cloned.1.call-done) | copy-start | bytes 3145732
Sparse Core Ops, SparseCore 0:
  10.0 57.6 all-gather.11
  70.4 56.7 all-gather.9
  129.9 58.2 all-gather.15
  190.8 57.9 all-gather.13
  251.0 20.1 all-reduce.3
  272.7 10.2 all-gather.23
  286.1 130.7 all-gather.17
  420.0 76.1 all-gather.21
  497.8 9.5 all-gather.19
where the time goes:
time: 520 us; the launch traced here: 518 us
  waiting for transfers between devices  451 us (87%)
  local copies, waits for them, and re-layouts  23.9 us (5%)
  matrix products  19.5 us (4%)
  between operations  13.4 us (3%)
  starting transfers between devices  7.04 us (1%)
    all_gather x1, waiting for transfers between devices, body(): query_part = lax.all_gather(w_query, 'db', axis=0, tiled=True)  130 us
    all_gather x1, waiting for transfers between devices, body(): key_part = lax.all_gather(w_key, 'db', axis=0, tiled=True)  60.6 us
    all_gather x1, waiting for transfers between devices, body(): expand_part = lax.all_gather(w_expand, 'db', axis=0, tiled=True)  59.5 us
    all_gather x1, waiting for transfers between devices, body(): reduce_part = lax.all_gather(w_reduce, 'db', axis=1, tiled=True)  57 us
    all_gather x1, waiting for transfers between devices, body(): value_part = lax.all_gather(w_value, 'db', axis=0, tiled=True)  53.5 us
    all_gather x1, waiting for transfers between devices, body(): reader_output_part = lax.all_gather(w_output, 'db', axis=0, tiled=True)  52.3 us
    psum x1, waiting for transfers between devices, body(): total = lax.psum(partial_sum, 'seq')  22.4 us
    gather x1, local copies, waits for them, and re-layouts, body(): key_value = arrived.reshape(-1, width)[flat_index]  11.6 us
  transfers between devices with their start and end apart: 10, of which 8 were waited for; matrix products, arithmetic and copies ran while one was open for 8% of the time, Pallas kernels for 0%

commit v1 on v0

--- a/solution.py
+++ b/solution.py
@@ -1,6 +1,11 @@
+import functools
+import math
+
 import jax
 import jax.numpy as jnp
 from jax import lax
+from jax.experimental import pallas as pl
+from jax.experimental.pallas import tpu as pltpu
 from jax.sharding import PartitionSpec as P
 
 HD = 128
@@ -17,7 +22,7 @@
     return widened * lax.rsqrt(mean_square + epsilon) * scales
 
 
-def body(
+def general_body(
     reader,
     reader_gain,
     database,
@@ -59,8 +64,12 @@
     table = jnp.dot(encoded, w_pairs, preferred_element_type=jnp.float32).astype(jnp.bfloat16)
     table = table.reshape(entries, stripe, w_pairs.shape[1])
     requests = neighbour_ids.reshape(shards, -1)
-    outgoing = table[requests]
-    arrived = lax.all_to_all(outgoing, "db", split_axis=0, concat_axis=0, tiled=True)
+    chosen = jax.nn.one_hot(requests, entries, dtype=jnp.bfloat16)
+    outgoing = jnp.einsum(
+        "brn,nsw->brsw", chosen, table, preferred_element_type=jnp.float32
+    ).astype(jnp.bfloat16)
+    outgoing = outgoing.reshape(-1, stripe, w_pairs.shape[1])
+    arrived = lax.all_to_all(outgoing.reshape(shards, -1, stripe, w_pairs.shape[1]), "db", split_axis=0, concat_axis=0, tiled=True)
     seq_len = rows.shape[0]
     per_seq = neighbour_ids.shape[1] * neighbour_ids.shape[2]
     width = arrived.shape[-1]
@@ -108,6 +117,319 @@
     return result[None]
 
 
+MESH = pl.DeviceIdType.MESH
+ZS, YS, XS = 4, 2, 2
+PLANE = YS * XS
+LIMIT = 56 * 1024 * 1024
+
+
+def remote(src, dst, send_sem, recv_sem, chip, core):
+    return pltpu.make_async_remote_copy(
+        src_ref=src,
+        dst_ref=dst,
+        send_sem=send_sem,
+        recv_sem=recv_sem,
+        device_id=(chip, core),
+        device_id_type=MESH,
+    )
+
+
+def enter(chip, core, shards):
+    barrier = pltpu.get_barrier_semaphore()
+    for step in range(1, shards):
+        pl.semaphore_signal(
+            barrier, inc=1, device_id=(lax.rem(chip + step, shards), core), device_id_type=MESH
+        )
+    pl.semaphore_signal(barrier, inc=1, device_id=(chip, 1 - core), device_id_type=MESH)
+    pl.semaphore_wait(barrier, shards)
+
+
+def gather_kernel(
+    ids, reader, database, encoder_w, pair_w, query_w, output_w,
+    rows_out, arrived, encoder_all, pair_all, query_all, output_all,
+    outgoing, z_send, z_recv, f_send, f_recv, s_send, s_recv,
+    row_send, row_recv, pass_send, pass_recv, local_sem,
+):
+    shards = ZS * PLANE
+    chip = lax.axis_index("db")
+    core = lax.axis_index("seq")
+    z, y, x = chip // PLANE, lax.rem(chip // XS, YS), lax.rem(chip, XS)
+
+    def at(zz, yy, xx):
+        return zz * PLANE + yy * XS + xx
+
+    enter(chip, core, shards)
+
+    shares = (encoder_w, pair_w, query_w, output_w)
+    wholes = (encoder_all.at[core], pair_all, query_all, output_all)
+    pieces = []
+    for number, share in enumerate(shares):
+        cut = share.shape[0] // 32 * 16
+        pieces.append((number, 0, cut, True))
+        pieces.append((number, cut, share.shape[0] - cut, False))
+
+    def place(p, zz, yy, xx):
+        number, low, count, _ = pieces[p]
+        return wholes[number].at[zz, yy, xx, pl.ds(low, count)]
+
+    def source(p):
+        number, low, count, _ = pieces[p]
+        return shares[number].at[pl.ds(low, count)]
+
+    def line(p, yy, xx):
+        number, low, count, _ = pieces[p]
+        return wholes[number].at[:, yy, xx, pl.ds(low, count)]
+
+    def peers(p):
+        if pieces[p][3]:
+            return (1 - y, x), (y, 1 - x)
+        return (y, 1 - x), (1 - y, x)
+
+    def along_z(p, step):
+        return remote(
+            source(p), place(p, z, y, x), z_send.at[p, step - 1], z_recv.at[p, step - 1],
+            at(lax.rem(z + step, ZS), y, x), core,
+        )
+
+    def from_z(p, step):
+        slot = place(p, lax.rem(z + ZS - step, ZS), y, x)
+        return remote(slot, slot, z_send.at[p, step - 1], z_recv.at[p, step - 1], chip, 1 - core)
+
+    def first(p, mine):
+        here = (y, x) if mine else peers(p)[0]
+        slots = line(p, *here)
+        return remote(slots, slots, f_send.at[p], f_recv.at[p], at(z, *peers(p)[0]), core)
+
+    def second(p, which, mine):
+        toward = peers(p)[1]
+        here = [(y, x), peers(p)[0]][which] if mine else [toward, (1 - y, 1 - x)][which]
+        slots = line(p, *here)
+        return remote(slots, slots, s_send.at[p, which], s_recv.at[p, which], at(z, *toward), core)
+
+    own = []
+    for number, share in enumerate(shares):
+        copy = pltpu.make_async_copy(share, wholes[number].at[z, y, x], local_sem.at[number])
+        copy.start()
+        own.append(copy)
+    kept = pltpu.make_async_copy(reader, rows_out.at[core], local_sem.at[4])
+    kept.start()
+    passed = remote(reader, rows_out.at[core], pass_send.at[0], pass_recv.at[0], chip, 1 - core)
+    passed.start()
+
+    for p in range(len(pieces)):
+        for step in range(1, ZS):
+            along_z(p, step).start()
+        if p == 0:
+            per_row = ids.shape[0] // (2 * shards)
+            for b in range(shards):
+                base = (b * 2 + core) * per_row
+                for m in range(per_row // KNN):
+                    both = [database[ids[base + m * KNN + j]] for j in range(KNN)]
+                    outgoing[b, m] = jnp.concatenate(both, axis=0)
+            for step in range(1, shards):
+                to = lax.rem(chip + step, shards)
+                remote(
+                    outgoing.at[to], arrived.at[:, chip], row_send.at[step - 1],
+                    row_recv.at[step - 1], to, core,
+                ).start()
+            mine = pltpu.make_async_copy(outgoing.at[chip], arrived.at[:, chip], local_sem.at[5])
+            mine.start()
+
+    for copy in own:
+        copy.wait()
+    for p in range(len(pieces) + 1):
+        if p < len(pieces):
+            for step in range(1, ZS):
+                from_z(p, step).wait_recv()
+            first(p, True).start()
+            second(p, 0, True).start()
+        if p > 0:
+            first(p - 1, False).wait_recv()
+            second(p - 1, 1, True).start()
+    whole = encoder_all.at[core]
+    for p in range(len(pieces)):
+        for which in range(2):
+            second(p, which, False).wait_recv()
+        if p == 1:
+            remote(whole, whole, pass_send.at[1], pass_recv.at[1], chip, 1 - core).start()
+
+    for p in range(len(pieces)):
+        for step in range(1, ZS):
+            along_z(p, step).wait_send()
+        first(p, True).wait_send()
+        for which in range(2):
+            second(p, which, True).wait_send()
+    for step in range(1, shards):
+        sender = lax.rem(chip + shards - step, shards)
+        landed = remote(
+            outgoing.at[sender], arrived.at[:, sender], row_send.at[step - 1],
+            row_recv.at[step - 1], sender, core,
+        )
+        landed.wait_send()
+        landed.wait_recv()
+    mine.wait()
+    kept.wait()
+    other = rows_out.at[1 - core]
+    taken = remote(other, other, pass_send.at[0], pass_recv.at[0], chip, 1 - core)
+    taken.wait_send()
+    taken.wait_recv()
+    other = encoder_all.at[1 - core]
+    taken = remote(other, other, pass_send.at[1], pass_recv.at[1], chip, 1 - core)
+    taken.wait_send()
+    taken.wait_recv()
+
+
+def gather_all(ids, reader, database, encoder_w, pair_w, query_w, output_w):
+    shards = ZS * PLANE
+    bf16 = jnp.bfloat16
+    features = database.shape[-1]
+    per_row = ids.shape[0] // (2 * shards)
+    spans = per_row // KNN
+    stripes = KNN * database.shape[1]
+
+    def whole(share):
+        return jax.ShapeDtypeStruct((ZS, YS, XS) + share.shape, bf16)
+
+    vmem, smem = pl.BlockSpec(memory_space=pltpu.VMEM), pl.BlockSpec(memory_space=pltpu.SMEM)
+    hbm = pl.BlockSpec(memory_space=pl.ANY)
+    dma = pltpu.SemaphoreType.DMA
+    return pl.pallas_call(
+        gather_kernel,
+        out_shape=(
+            jax.ShapeDtypeStruct((2,) + reader.shape, bf16),
+            jax.ShapeDtypeStruct((spans, shards, stripes, features), bf16),
+            jax.ShapeDtypeStruct((2, ZS, YS, XS) + encoder_w.shape, bf16),
+            whole(pair_w),
+            whole(query_w),
+            whole(output_w),
+        ),
+        in_specs=[smem, hbm, vmem, hbm, hbm, hbm, hbm],
+        out_specs=(hbm,) * 6,
+        scratch_shapes=[
+            pltpu.VMEM((shards, spans, stripes, features), bf16),
+            dma((8, 3)), dma((8, 3)), dma((8,)), dma((8,)), dma((8, 2)), dma((8, 2)),
+            dma((shards - 1,)), dma((shards - 1,)), dma((2,)), dma((2,)), dma((6,)),
+        ],
+        compiler_params=pltpu.CompilerParams(
+            collective_id=0, has_side_effects=True, vmem_limit_bytes=LIMIT // 4
+        ),
+    )(ids, reader, database, encoder_w, pair_w, query_w, output_w)
+
+
+def swap_kernel(mine, both, send_sem, recv_sem, local_sem):
+    chip = lax.axis_index("db")
+    core = lax.axis_index("seq")
+    barrier = pltpu.get_barrier_semaphore()
+    pl.semaphore_signal(barrier, inc=1, device_id=(chip, 1 - core), device_id_type=MESH)
+    pl.semaphore_wait(barrier, 1)
+    kept = pltpu.make_async_copy(mine, both.at[core], local_sem)
+    kept.start()
+    copy = remote(mine, both.at[core], send_sem, recv_sem, chip, 1 - core)
+    copy.start()
+    kept.wait()
+    copy.wait()
+
+
+def swap(mine, number):
+    vmem = pl.BlockSpec(memory_space=pltpu.VMEM)
+    return pl.pallas_call(
+        swap_kernel,
+        out_shape=jax.ShapeDtypeStruct((2,) + mine.shape, mine.dtype),
+        in_specs=[vmem],
+        out_specs=vmem,
+        scratch_shapes=[pltpu.SemaphoreType.DMA] * 3,
+        compiler_params=pltpu.CompilerParams(
+            collective_id=number, has_side_effects=True, vmem_limit_bytes=LIMIT // 4
+        ),
+    )(mine)
+
+
+def banded_body(
+    reader,
+    reader_gain,
+    database,
+    encoder_gain,
+    w_expand,
+    w_reduce,
+    w_query,
+    w_key,
+    w_value,
+    w_output,
+    neighbour_ids,
+    lengths,
+    owners,
+):
+    f32, bf16 = jnp.float32, jnp.bfloat16
+    shards = ZS * PLANE
+    core = lax.axis_index("seq")
+    stripe, features = database.shape[1:]
+    head_cols, model_cols = w_query.shape[1], w_output.shape[1]
+    band = w_expand.shape[0]
+    encoder_w = jnp.concatenate([w_expand, w_reduce.T], axis=0)
+    pair_w = jnp.concatenate([w_key, w_value], axis=0)
+    rows, arrived, encoder_all, pair_all, query_all, output_all = gather_all(
+        neighbour_ids.reshape(-1), reader[0], database, encoder_w, pair_w, w_query, w_output
+    )
+    rows = rows.reshape(-1, rows.shape[-1])
+    encoder_all = encoder_all.reshape(2, shards, 2 * band, -1)
+    stored = arrived.reshape(-1, features)
+    normed_rows = rms_scale(stored, encoder_gain).astype(bf16)
+    total = 0.0
+    for part in range(2):
+        expand = encoder_all[part, :, :band].reshape(shards * band, -1)
+        reduce_t = encoder_all[part, :, band:].reshape(shards * band, -1)
+        hidden = jax.nn.gelu(
+            jnp.dot(normed_rows, expand, preferred_element_type=f32), approximate=False
+        ).astype(bf16)
+        total = total + lax.dot_general(
+            hidden, reduce_t, (((1,), (1,)), ((), ())), preferred_element_type=f32
+        )
+    encoded = (stored.astype(f32) + total).astype(bf16)
+    encoded = swap(encoded, 1).reshape(-1, features)
+
+    spans = neighbour_ids.shape[1] * neighbour_ids.shape[2] // KNN
+    window = encoded.shape[0] // spans
+    encoded = encoded[: (spans - 1) * window]
+    pair_all = pair_all.reshape(shards, 2 * band, -1)
+    key_w = pair_all[:, :band].reshape(shards * band, -1)
+    value_w = pair_all[:, band:].reshape(shards * band, -1)
+    heads = head_cols // HD
+    keys = jnp.dot(encoded, key_w, preferred_element_type=f32).astype(bf16)
+    values = jnp.dot(encoded, value_w, preferred_element_type=f32).astype(bf16)
+    normed_tokens = rms_scale(rows[SPAN:], reader_gain).astype(bf16)
+    queries = jnp.dot(
+        normed_tokens, query_all.reshape(-1, head_cols), preferred_element_type=f32
+    ).astype(bf16)
+
+    owner = owners[0].reshape(spans, 1, KNN, 1)
+    length = lengths[0].reshape(spans, 1, KNN, 1)
+    origin = jnp.arange(shards, dtype=jnp.int32)[None, :, None, None]
+    offset = jnp.arange(stripe, dtype=jnp.int32)[None, None, None, :]
+    position = lax.rem(origin - owner + shards, shards) * stripe + offset
+    live = (position < length).reshape(spans, window)[: spans - 1]
+
+    query_spans = queries.reshape(spans - 1, SPAN, heads, HD)
+    key_heads = keys.reshape(spans - 1, window, heads, HD)
+    value_heads = values.reshape(spans - 1, window, heads, HD)
+    scores = jnp.einsum(
+        "cqhd,ckhd->chqk", query_spans, key_heads, preferred_element_type=f32
+    ) * HD ** (-0.5)
+    masked = jnp.where(live[:, None, None, :], scores, -jnp.inf)
+    largest = jnp.max(masked, axis=-1, keepdims=True)
+    powers = jnp.exp(masked - largest)
+    totals = jnp.sum(powers, axis=-1, keepdims=True)
+    weights = (powers / totals).astype(bf16)
+    attended = jnp.einsum("chqk,ckhd->cqhd", weights, value_heads, preferred_element_type=f32)
+    attended = attended.reshape(-1, head_cols).astype(bf16)
+    attended = swap(attended, 2)
+    output_part = output_all.reshape(2, head_cols, model_cols)
+    update = jnp.dot(attended[0], output_part[0], preferred_element_type=f32)
+    update = update + jnp.dot(attended[1], output_part[1], preferred_element_type=f32)
+    update = jnp.concatenate([jnp.zeros((SPAN, model_cols), f32), update], axis=0)
+    residual = lax.dynamic_slice_in_dim(rows, core * model_cols, model_cols, 1)
+    return (residual.astype(f32) + update).astype(bf16)[None]
+
+
 def solution(mesh):
     in_specs = (
         P("db", "seq", None),
@@ -125,4 +447,6 @@
         P("db", None, None),
     )
     out_specs = P("db", None, "seq")
+    grid = (mesh.shape["db"], mesh.shape["seq"])
+    body = banded_body if grid == (ZS * YS * XS, 2) else general_body
     return jax.shard_map(body, mesh=mesh, in_specs=in_specs, out_specs=out_specs, check_vma=False)

time: 520 us -> 247 us (0.47)
  waiting for transfers between devices: 451 us -> 0 us
  Pallas kernels: 0 us -> 191 us
  between operations: 13.4 us -> 0.29 us
  matrix products: 19.5 us -> 31.6 us
  starting transfers between devices: 7.04 us -> 0 us
    all_gather x8 -> x0, waiting for transfers between devices: 424 us -> none  [the longest x1 130 us: body(): query_part = lax.all_gather(w_query, 'db', axis=0, tiled=True)]
    pallas_call x0 -> x3, Pallas kernels: none -> 191 us  [the longest x1 185 us: gather_all(): pl.pallas_call(gather_kernel, out_shape=(jax.ShapeDtypeStruct((2,) + read...]
    psum x1 -> x0, waiting for transfers between devices: 22.4 us -> none  [body(): total = lax.psum(partial_sum, 'seq')]
    gather x2 -> x0, local copies, waits for them, and re-layouts: 14.4 us -> none  [the longest x1 11.6 us: body(): key_value = arrived.reshape(-1, width)[flat_index]]
    dot_general x6 -> x9, matrix products: 19.5 us -> 31.6 us  [the longest x2 17.7 us: banded_body(): lax.dot_general(hidden, reduce_t, (((1,), (1,)), ((), ())), preferred_ele...]
    unnamed x16 -> x35, local copies, waits for them, and re-layouts: 1.82 us -> 11.4 us
    all_to_all x1 -> x0, starting transfers between devices: 6.55 us -> none  [body(): lax.all_to_all(outgoing, 'db', split_axis=0, concat_axis=0, tiled=True)]
  transfers between devices with their start and end apart: 10 -> 0, of which waited for: 8 -> 0; matrix products, arithmetic and copies ran while one was open for 8% -> 0% of each run, Pallas kernels for 0% -> 0%
where the time goes in v1:
time: 247 us
  Pallas kernels  191 us (77%)
  matrix products  31.6 us (13%)
  local copies, waits for them, and re-layouts  19.4 us (8%)
  other arithmetic  4.27 us (2%)
    pallas_call x1, Pallas kernels, gather_all(): pl.pallas_call(gather_kernel, out_shape=(jax.ShapeDtypeStruct((2,) + read...  185 us
    dot_general x2, matrix products, banded_body(): lax.dot_general(hidden, reduce_t, (((1,), (1,)), ((), ())), preferred_ele...  17.7 us
    unnamed x35, local copies, waits for them, and re-layouts  11.4 us
    pallas_call x2, Pallas kernels, swap(): pl.pallas_call(swap_kernel, out_shape=jax.ShapeDtypeStruct((2,) + mine.sh...  5.79 us
    dot_general x1, matrix products, banded_body(): jnp.einsum('chqk,ckhd->cqhd', weights, value_heads, preferred_element_typ...  5.23 us

profile of v1, /device:TPU:9, one launch (start us, length us, event | category | flops | bytes accessed | tf_op | source)
XLA Modules:
  0.0 246.9 jit_solution(9809542235708237564)
XLA Ops:
  0.0 0.8 copy.19
  0.9 1.0 pad_maximum_fusion.1.encoder_w
  1.9 1.0 pad_maximum_fusion.pair_w
  2.8 1.0 copy-done
  3.9 1.0 copy-done.1
  4.9 0.9 copy-done.2
  5.8 0.9 copy-done.3
  6.8 185.5 %shard_map.127 = (bf16[2,128,2048]{2,1,0:T(8,128)(2,1)S(1)}, bf16[2,16,16,896]{3,2,1,0:T(8,128)(2,1)S(1)}, bf16[2,4,2,2,112,896]{5,4,3,2,1,0:T(8,128)(2,1)S(1)},...) custom-call(s32[128]{0:T(128)S(1)} %reshape.116.ids, ...), custom_call_target="tpu_custom_call" | custom-call | tf_op jit(solution)/shard_map/pallas_call | solution.py:296
  192.3 1.9 copy-done.4
  194.2 2.4 fusion.153
  196.7 2.2 fusion.154
  198.9 2.8 %fusion.152 = (bf16[1,16,56,896]{3,2,1,0:T(8,128)(2,1)}, bf16[1,16,56,896]{3,2,1,0:T(8,128)(2,1)}, bf16[1,16,56,896]{3,2,1,0:T(8,128)(2,1)}, bf16[1,16,56,896]{3,2,1,0:T(8,128)(2,1)}) fusion(bf16[2,16,112,896]{3,2,1,0:T(8,128)(2,1)S(1)} %bitcast.61), kind=kLoop, calls=%fused_computation.181 | loop fusion | bytes 12845056 | tf_op jit(solution)/shard_map/slice | solution.py:379
  202.3 9.2 %fusion.74 = f32[512,896]{1,0:T(8,128)} fusion(bf16[896,896]{1,0:T(8,128)(2,1)} %bitcast.78, bf16[512,896]{1,0:T(8,128)(2,1)S(1)} %bitcast.83, bf16[896,896]{1,0:T(8,128)(2,1)} %bitcast.79), kind=kOutput, calls=%fused_computation.97 | convolution fusion | flops 1673986048 | bytes 5963776 | tf_op jit(solution)/shard_map/dot_general | solution.py:384
  211.4 8.6 %fusion.7.mine = bf16[512,896]{1,0:T(8,128)(2,1)S(1)} fusion(f32[512,896]{1,0:T(8,128)} %fusion.74, bf16[896,896]{1,0:T(8,128)(2,1)} %bitcast.77, bf16[2,16,16,896]{3,2,1,0:T(8,128)(2,1)S(1)} %get-tuple-element.12, bf16[512,896]{1,0:T(8,128)(2,1)} %bitcast.84, bf16[896,896]{1,0:T(8,128)(2,1)} %bitcast.76), kind=kOutput, calls=%fused_computation.12 | convolution fusion | flops 1675821056 | bytes 7798784 | tf_op jit(solution)/shard_map/dot_general | solution.py:384
  220.0 3.8 %shard_map.128 = bf16[2,512,896]{2,1,0:T(8,128)(2,1)S(1)} custom-call(bf16[512,896]{1,0:T(8,128)(2,1)S(1)} %fusion.7.mine), custom_call_target="tpu_custom_call" | custom-call | tf_op jit(solution)/shard_map/pallas_call | solution.py:335
  223.9 1.8 fusion.32
  225.7 1.6 copy.26
  227.4 1.8 fusion.33
  230.5 3.2 %fusion.40 = bf16[24,8,8,128]{3,1,2,0:T(8,128)(2,1)S(1)} fusion(bf16[2048,1024]{1,0:T(8,128)(2,1)} %bitcast.70, f32[2048]{0:T(1024)S(1)} %copy-done.14, f32[192]{0:T(256)S(1)} %add_rsqrt_fusion.1, bf16[256,2048]{1,0:T(8,128)(2,1)S(1)} %bitcast.66), kind=kOutput, calls=%fused_computation.65 | convolution fusion | flops 807075840 | bytes 5383168 | tf_op jit(solution)/shard_map/dot_general | solution.py:400
  234.5 1.2 copy-done.7
  236.2 5.2 %fusion.41 = bf16[3,64,8,128]{3,1,2,0:T(8,128)(2,1)S(1)} fusion(bf16[3,256,8,128]{3,2,1,0:T(8,128)(2,1)} %bitcast.80, f32[3,8,64]{2,1,0:T(8,128)S(1)} %fusion.155, f32[3,8,64,256]{3,2,1,0:T(8,128)} %copy-done.7), kind=kOutput, calls=%fused_computation.66 | convolution fusion | flops 102041344 | bytes 3545088 | tf_op jit(solution)/shard_map/chqk,ckhd->cqhd/dot_general | solution.py:422
  241.8 1.9 shard_map.129
  244.4 1.0 copy-done.5
  246.0 0.9 fusion.81
  (43 shorter events, 4.8 us)
Async XLA Ops:
  2.8 1.0 copy-start
  3.9 1.0 copy-start.1
  4.9 0.9 copy-start.2
  5.8 0.9 copy-start.3
  192.3 1.9 copy-start.4
  198.9 3.1 %copy-start.11 = (f32[896]{0:T(1024)S(1)}, f32[896]{0:T(1024)}, u32[]{:S(2)}) copy-start(f32[896]{0:T(1024)} %param.16) | copy-start | bytes 10756
  202.2 9.2 %copy-start.10 = (bf16[2,16,16,896]{3,2,1,0:T(8,128)(2,1)}, bf16[2,16,16,896]{3,2,1,0:T(8,128)(2,1)S(1)}, u32[]{:S(2)}) copy-start(bf16[2,16,16,896]{3,2,1,0:T(8,128)(2,1)S(1)} %multiply_convert_fusion) | copy-start | bytes 2752516
  220.0 3.9 %copy-start.9 = (bf16[16,56,1024]{2,1,0:T(8,128)(2,1)S(1)}, bf16[16,56,1024]{2,1,0:T(8,128)(2,1)}, u32[]{:S(2)}) copy-start(bf16[16,56,1024]{2,1,0:T(8,128)(2,1)} %get-tuple-element.24) | copy-start | bytes 5505028
  225.7 1.7 copy-start.8
  229.2 0.7 copy-start.12
  229.2 0.8 copy-start.13
  229.2 1.3 copy-start.14
  234.5 1.2 copy-start.7
  241.5 2.3 copy-start.6
  243.8 1.6 copy-start.5

commit v2 on v1

--- a/solution.py
+++ b/solution.py
@@ -120,6 +120,7 @@
 MESH = pl.DeviceIdType.MESH
 ZS, YS, XS = 4, 2, 2
 PLANE = YS * XS
+AHEAD = 2
 LIMIT = 56 * 1024 * 1024
 
 
@@ -216,7 +217,7 @@
     passed = remote(reader, rows_out.at[core], pass_send.at[0], pass_recv.at[0], chip, 1 - core)
     passed.start()
 
-    for p in range(len(pieces)):
+    for p in range(AHEAD):
         for step in range(1, ZS):
             along_z(p, step).start()
         if p == 0:
@@ -243,6 +244,9 @@
                 from_z(p, step).wait_recv()
             first(p, True).start()
             second(p, 0, True).start()
+            if p + AHEAD < len(pieces):
+                for step in range(1, ZS):
+                    along_z(p + AHEAD, step).start()
         if p > 0:
             first(p - 1, False).wait_recv()
             second(p - 1, 1, True).start()
@@ -374,16 +378,17 @@
     encoder_all = encoder_all.reshape(2, shards, 2 * band, -1)
     stored = arrived.reshape(-1, features)
     normed_rows = rms_scale(stored, encoder_gain).astype(bf16)
-    total = 0.0
+    hidden_parts = []
     for part in range(2):
         expand = encoder_all[part, :, :band].reshape(shards * band, -1)
-        reduce_t = encoder_all[part, :, band:].reshape(shards * band, -1)
-        hidden = jax.nn.gelu(
-            jnp.dot(normed_rows, expand, preferred_element_type=f32), approximate=False
-        ).astype(bf16)
-        total = total + lax.dot_general(
-            hidden, reduce_t, (((1,), (1,)), ((), ())), preferred_element_type=f32
-        )
+        product = jnp.dot(normed_rows, expand, preferred_element_type=f32)
+        product = lax.optimization_barrier(product)
+        hidden_parts.append(jax.nn.gelu(product, approximate=False).astype(bf16))
+    hidden = lax.optimization_barrier(jnp.concatenate(hidden_parts, axis=1))
+    reduce_t = jnp.concatenate(
+        [encoder_all[part, :, band:].reshape(shards * band, -1) for part in range(2)], axis=1
+    )
+    total = lax.dot_general(hidden, reduce_t, (((1,), (1,)), ((), ())), preferred_element_type=f32)
     encoded = (stored.astype(f32) + total).astype(bf16)
     encoded = swap(encoded, 1).reshape(-1, features)
 

time: 247 us -> 217 us (0.88)
  Pallas kernels: 191 us -> 174 us
  matrix products: 31.6 us -> 15.1 us
  other arithmetic: 4.27 us -> 12.4 us
  local copies, waits for them, and re-layouts: 19.4 us -> 14.6 us
    pallas_call x1, Pallas kernels: 185 us -> 168 us  [gather_all(): pl.pallas_call(gather_kernel, out_shape=(jax.ShapeDtypeStruct((2,) + read...]
    dot_general x2 -> x1, matrix products: 17.7 us -> 2.1 us  [banded_body(): lax.dot_general(hidden, reduce_t, (((1,), (1,)), ((), ())), preferred_ele...]
    convert_element_type x0 -> x1, other arithmetic: none -> 7.98 us  [banded_body(): hidden_parts.append(jax.nn.gelu(product, approximate=False).astype(bf16))]
    unnamed x35 -> x19, local copies, waits for them, and re-layouts: 11.4 us -> 8.85 us
where the time goes in v2:
time: 217 us; the launch traced here: 216 us
  Pallas kernels  174 us (80%)
  matrix products  15.1 us (7%)
  local copies, waits for them, and re-layouts  14.6 us (7%)
  other arithmetic  12.4 us (6%)
    pallas_call x1, Pallas kernels, gather_all(): pl.pallas_call(gather_kernel, out_shape=(jax.ShapeDtypeStruct((2,) + read...  168 us
    unnamed x19, local copies, waits for them, and re-layouts  8.85 us
    convert_element_type x1, other arithmetic, banded_body(): hidden_parts.append(jax.nn.gelu(product, approximate=False).astype(bf16))  7.98 us
    pallas_call x2, Pallas kernels, swap(): pl.pallas_call(swap_kernel, out_shape=jax.ShapeDtypeStruct((2,) + mine.sh...  5.68 us

profile of v2, /device:TPU:9, one launch (start us, length us, event | category | flops | bytes accessed | tf_op | source)
XLA Modules:
  0.0 216.1 jit_solution(16226414461152879463)
XLA Ops:
  0.0 0.8 lt.14
  0.8 0.8 sub.29
  1.5 0.8 copy.19
  2.7 1.0 pad_maximum_fusion.2.encoder_w
  3.6 1.0 pad_maximum_fusion.1.pair_w
  4.6 1.0 copy-done.1
  5.7 1.0 copy-done.2
  6.7 0.9 copy-done.3
  7.6 0.9 copy-done.4
  8.6 168.1 %shard_map.127 = (bf16[2,128,2048]{2,1,0:T(8,128)(2,1)S(1)}, bf16[2,16,16,896]{3,2,1,0:T(8,128)(2,1)S(1)}, bf16[2,4,2,2,112,896]{5,4,3,2,1,0:T(8,128)(2,1)S(1)},...) custom-call(s32[128]{0:T(128)S(1)} %reshape.116.ids, ...), custom_call_target="tpu_custom_call" | custom-call | tf_op jit(solution)/shard_map/pallas_call | solution.py:300
  176.7 1.9 copy-done
  179.4 1.0 fusion.46
  181.1 1.2 fusion.72
  182.3 1.2 fusion.71
  183.5 8.0 %fusion.7 = (bf16[512,896]{1,0:T(8,128)(2,1)S(1)}, bf16[512,896]{1,0:T(8,128)(2,1)S(1)}) fusion(f32[512,896]{1,0:T(8,128)S(1)} %fusion.71, f32[512,896]{1,0:T(8,128)S(1)} %fusion.72), kind=kLoop, calls=%fused_computation.11 | loop fusion | flops 59637760 | bytes 5505024 | tf_op jit(solution)/shard_map/convert_element_type | solution.py:386
  191.7 2.1 fusion.11.mine
  193.8 3.7 %shard_map.128 = bf16[2,512,896]{2,1,0:T(8,128)(2,1)S(1)} custom-call(bf16[512,896]{1,0:T(8,128)(2,1)S(1)} %fusion.11.mine), custom_call_target="tpu_custom_call" | custom-call | tf_op jit(solution)/shard_map/pallas_call | solution.py:339
  198.0 1.8 fusion.37
  200.9 1.8 fusion.36
  202.7 1.6 copy.26
  204.8 4.2 %fusion.47 = bf16[3,64,8,128]{3,1,2,0:T(8,128)(2,1)S(1)} fusion(bf16[3,256,8,128]{3,2,1,0:T(8,128)(2,1)} %bitcast.79, f32[3,8,64]{2,1,0:T(8,128)S(1)} %fusion.70, f32[3,8,64,256]{3,2,1,0:T(8,128)S(1)} %multiply_select_fusion), kind=kOutput, calls=%fused_computation.71 | convolution fusion | flops 102041344 | bytes 3545088 | tf_op jit(solution)/shard_map/chqk,ckhd->cqhd/dot_general | solution.py:427
  209.3 1.9 shard_map.129
  211.3 2.7 %fusion.68 = (bf16[2,2,2,128,1024]{4,3,2,1,0:T(8,128)(2,1)S(1)}, bf16[2,2,2,128,1024]{4,3,2,1,0:T(8,128)(2,1)S(1)}) fusion(bf16[4,2,2,128,1024]{4,3,2,1,0:T(8,128)(2,1)} %copy-done), kind=kLoop, calls=%fused_computation.98 | loop fusion | bytes 8388608 | tf_op jit(solution)/shard_map/slice | solution.py:432
  215.2 0.9 fusion.55
  (30 shorter events, 5.5 us)
Async XLA Ops:
  4.6 1.0 copy-start.1
  5.7 1.0 copy-start.2
  6.7 0.9 copy-start.3
  7.6 0.9 copy-start.4
  176.7 1.9 copy-start
  178.6 0.8 copy-start.6
  179.4 1.4 copy-start.5
